TPU v7x, 32 devices: a whole 2x2x4 slice. The times are simulated.
32 devices in a mesh: dp: 8 (over z, core), neuron: 4 (over y, x).
Axes of the slice: x: 2, y: 2, z: 4, core: 2. Of those that a mesh axis runs over, the one named last changes fastest.
Arguments:
- acts_a: bfloat16 [4096, 4096], P('dp'), may hold values from -150 to 150
- acts_b: bfloat16 [4096, 4096], P('dp'), may hold values from -150 to 150
- grads_a: bfloat16 [4096, 14336], P('dp', 'neuron'), may hold values from -150 to 150
- grads_b: bfloat16 [4096, 14336], P('dp', 'neuron'), may hold values from -150 to 150
- weights_a: bfloat16 [4096, 14336], P('dp', 'neuron'), may hold values from -6 to 6
- weights_b: bfloat16 [4096, 14336], P('dp', 'neuron'), may hold values from -6 to 6
- block_match: int32 [112], replicated, may hold values from 0 to 111, as said below
Outputs:
- merged: float32 [4096, 14336], P('dp', 'neuron')
Inputs may be any that keep to these rules, and one draw needn't show every extreme that they name: `block_match`: A permutation of the 112 blocks. For any two indices s and t of neuron (s may equal t), at most 7 of the 28 blocks held by s is matched to a position held by t; so each index receives its 28 matched blocks from 28 different indices, one of them itself.
All inputs are finite; a program needn't handle non-finite values.
Results may differ from a plain program's by a relative error of at most 0.0003.
Values may be sent and summed in bfloat16 or wider, within the bound.
A program may use at most 256 MiB of HBM per device.

v0:
```python
import jax
import jax.numpy as jnp
from jax import lax
from jax.sharding import PartitionSpec as P

BLK = 128


EPSILON = 1e-06


def squared(values):
    wide = values.astype(jnp.float32)
    return (wide * wide).astype(jnp.bfloat16)


def block_plan(block_match, my_index, per_dev, capacity):
    total = block_match.shape[0]
    global_ids = jnp.arange(total, dtype=jnp.int32)
    hits = block_match[None, :] == global_ids[:, None]
    target = jnp.sum(jnp.where(hits, global_ids[None, :], 0), axis=1)
    target_dev = target // per_dev
    source_dev = global_ids // per_dev
    local_ids = global_ids % per_dev
    earlier = (
        (source_dev[:, None] == source_dev[None, :])
        & (target_dev[:, None] == target_dev[None, :])
        & (local_ids[None, :] < local_ids[:, None])
    )
    ranked = jnp.sum(earlier.astype(jnp.int32), axis=1)
    send_all = target_dev * capacity + ranked
    send_slot = lax.dynamic_slice_in_dim(send_all, my_index * per_dev, per_dev)
    wanted = lax.dynamic_slice_in_dim(block_match, my_index * per_dev, per_dev)
    recv_slot = wanted // per_dev * capacity + jnp.take(ranked, wanted)
    return (send_slot, recv_slot, wanted)


def pack_blocks(data, send_slot, slots):
    rows = data.shape[0]
    split = data.reshape(rows, -1, BLK)
    empty = jnp.zeros((rows, slots, BLK), data.dtype)
    return empty.at[:, send_slot, :].set(split)


def unpack_blocks(received, recv_slot):
    picked = jnp.take(received, recv_slot, axis=1)
    return picked.reshape(received.shape[0], -1)


def term_maker(sq_acts, sq_grads):
    return lax.dot_general(
        sq_acts, sq_grads, (((0,), (0,)), ((), ())), preferred_element_type=jnp.float32
    )


def on_device(acts_a, acts_b, grads_a, grads_b, weights_a, weights_b, block_match):
    neurons = lax.axis_size("neuron")
    my_index = lax.axis_index("neuron")
    per_dev = grads_b.shape[1] // BLK
    capacity = (per_dev + neurons - 1) // neurons
    slots = neurons * capacity
    send_slot, recv_slot, wanted = block_plan(block_match, my_index, per_dev, capacity)
    sq_grads_a = squared(grads_a)
    sq_grads_b = squared(grads_b)
    sq_acts_a = squared(acts_a)
    sq_acts_b = squared(acts_b)
    fisher_a = lax.psum_scatter(
        term_maker(sq_acts_a, sq_grads_a), "dp", scatter_dimension=0, tiled=True
    )
    fisher_b = lax.psum_scatter(
        term_maker(sq_acts_b, sq_grads_b), "dp", scatter_dimension=0, tiled=True
    )
    moved_fisher = lax.all_to_all(
        pack_blocks(fisher_b, send_slot, slots), "neuron", split_axis=1, concat_axis=1, tiled=True
    )
    fisher_b = unpack_blocks(moved_fisher, recv_slot)
    moved_weight = lax.all_to_all(
        pack_blocks(weights_b, send_slot, slots), "neuron", split_axis=1, concat_axis=1, tiled=True
    )
    weights_match = unpack_blocks(moved_weight, recv_slot)
    wide_a = weights_a.astype(jnp.float32)
    wide_b = weights_match.astype(jnp.float32)
    return (fisher_a * wide_a + fisher_b * wide_b) / (fisher_a + fisher_b + EPSILON)


def solution(mesh):
    placed = (
        P("dp", None),
        P("dp", None),
        P("dp", "neuron"),
        P("dp", "neuron"),
        P("dp", "neuron"),
        P("dp", "neuron"),
        P(),
    )
    return jax.shard_map(
        on_device, mesh=mesh, in_specs=placed, out_specs=P("dp", "neuron"), check_vma=False
    )
```

profile of v0, /device:TPU:0, one launch (start us, length us, event | category | flops | bytes accessed | tf_op | source)
XLA Modules:
  0.0 1179.5 jit_solution(12361314383646823421)
XLA Ops:
  6.5 0.0 reduce-scatter.5.cloned.1.call-start
  6.5 26.7 %fusion.1 = f32[4096,3584]{1,0:T(8,128)} fusion(bf16[512,4096]{1,0:T(8,128)(2,1)} %param.8, bf16[512,3584]{1,0:T(8,128)(2,1)} %param.10), kind=kOutput, calls=%fused_computation.11 | convolution fusion | flops 15044182016 | bytes 66584576 | tf_op jit(solution)/shard_map/dot_general | solution.py:51
  33.3 0.0 reduce-scatter.5.cloned.1.call-update
  33.3 0.2 reduce-scatter.3.cloned.1.call-start
  33.5 27.9 %fusion = f32[4096,3584]{1,0:T(8,128)} fusion(bf16[512,4096]{1,0:T(8,128)(2,1)} %param.7, bf16[512,3584]{1,0:T(8,128)(2,1)} %param.9), kind=kOutput, calls=%fused_computation.10 | convolution fusion | flops 15044182016 | bytes 66584576 | tf_op jit(solution)/shard_map/dot_general | solution.py:51
  61.4 0.0 reduce-scatter.3.cloned.1.call-update
  61.4 0.0 copy-start
  61.4 6.0 copy.24
  67.4 6.0 copy.25
  73.4 0.0 copy-done
  73.4 0.1 select_reduce_fusion
  73.5 0.2 convert_reduce_fusion
  73.7 0.1 compare_select_fusion
  73.8 2.7 broadcast_in_dim.69
  76.5 11.1 scatter_fusion.1
  87.5 4.7 all-to-all-start.1
  92.3 505.8 %reduce-scatter.5.cloned.1.call-done = f32[512,3584]{1,0:T(8,128)} async-done(((f32[4096,3584]{1,0:T(8,128)}), f32[512,3584]{1,0:T(8,128)}) %reduce-scatter.5.cloned.1.call-update) | async-done | bytes 7340048 | tf_op jit(solution)/shard_map/reduce_scatter | solution.py:70
  598.1 8.4 copy.20
  606.4 8.4 copy.21
  614.9 3.9 broadcast_in_dim.65
  618.7 14.7 %scatter_fusion = f32[512,28,128]{2,0,1:T(8,128)} fusion(f32[512,28,128]{2,0,1:T(8,128)} %broadcast_in_dim.65, s32[28]{0:T(128)S(1)} %compare_select_fusion, f32[28,512,128]{2,1,0:T(8,128)} %copy.21), kind=kCustom, calls=%fused_computation.3 | custom fusion | bytes 22020208 | tf_op jit(solution)/shard_map/scatter | solution.py:42
  633.5 0.0 all-to-all-done.1
  633.5 5.7 all-to-all-start
  639.1 0.1 compare_select_fusion.2
  639.2 0.7 gather_fusion
  639.9 0.1 compare_and_fusion
  640.0 0.1 broadcast_bitcast_fusion
  640.1 5.0 gather_fusion.2
  645.1 5.9 copy.26
  651.0 6.0 copy.27
  657.0 61.4 %all-to-all-done = f32[512,28,128]{2,0,1:T(8,128)} async-done(((f32[512,28,128]{2,0,1:T(8,128)}), f32[512,28,128]{2,0,1:T(8,128)}, u32[]{:S(2)}, u32[]{:S(2)}) %all-to-all-start) | async-done | bytes 7340064 | tf_op jit(solution)/shard_map/all_to_all | solution.py:73
  718.4 7.2 gather_fusion.1
  725.6 8.4 copy.22
  734.0 8.5 copy.23
  742.5 418.3 %reduce-scatter.3.cloned.1.call-done = f32[512,3584]{1,0:T(8,128)} async-done(((f32[4096,3584]{1,0:T(8,128)}), f32[512,3584]{1,0:T(8,128)}) %reduce-scatter.3.cloned.1.call-update) | async-done | bytes 7340048 | tf_op jit(solution)/shard_map/reduce_scatter | solution.py:67
  1160.8 11.8 add_divide_fusion
  (5 shorter events, 0.1 us)
Async XLA Ops:
  6.5 591.5 %reduce-scatter.5.cloned.1.call-start = ((), (), s32[]{:S(2)}) async-start(), calls=%async_computation.5 | async-start | bytes 66060288 | tf_op jit(solution)/shard_map/reduce_scatter | solution.py:70
  33.3 1127.6 %reduce-scatter.3.cloned.1.call-start = ((), (), s32[]{:S(2)}) async-start(), calls=%async_computation.4 | async-start | bytes 66060288 | tf_op jit(solution)/shard_map/reduce_scatter | solution.py:67
  61.4 12.0 %copy-start = (s32[112]{0:T(128)S(1)}, s32[112]{0:T(128)}, u32[]{:S(2)}) copy-start(s32[112]{0:T(128)} %param.13) | copy-start | bytes 1348
  87.5 545.9 %all-to-all-start.1 = ((bf16[512,28,128]{2,0,1:T(8,128)(2,1)}), bf16[512,28,128]{2,0,1:T(8,128)(2,1)}, u32[]{:S(2)}, u32[]{:S(2)}) async-start(bf16[512,28,128]{2,0,1:T(8,128)(2,1)} %scatter_fusion.1), calls=%async_computation.3 | async-start | bytes 7340032 | tf_op jit(solution)/shard_map/all_to_all | solution.py:77
  633.5 84.9 %all-to-all-start = ((f32[512,28,128]{2,0,1:T(8,128)}), f32[512,28,128]{2,0,1:T(8,128)}, u32[]{:S(2)}, u32[]{:S(2)}) async-start(f32[512,28,128]{2,0,1:T(8,128)} %scatter_fusion), calls=%async_computation.2 | async-start | bytes 14680064 | tf_op jit(solution)/shard_map/all_to_all | solution.py:73
Sparse Core Ops, SparseCore 0:
  33.4 564.6 reduce-scatter.4
  600.6 560.2 reduce-scatter.2
where the time goes:
time: 1180 us
  waiting for transfers between devices  986 us (84%)
  local copies, waits for them, and re-layouts  103 us (9%)
  matrix products  54.6 us (5%)
  between operations  13.5 us (1%)
  other arithmetic  12.4 us (1%)
    reduce_scatter x1, waiting for transfers between devices, on_device(): lax.psum_scatter(term_maker(sq_acts_b, sq_grads_b), 'dp', scatter_dimensi...  506 us
    reduce_scatter x1, waiting for transfers between devices, on_device(): lax.psum_scatter(term_maker(sq_acts_a, sq_grads_a), 'dp', scatter_dimensi...  418 us
    all_to_all x1, waiting for transfers between devices, on_device(): lax.all_to_all(pack_blocks(fisher_b, send_slot, slots), 'neuron', split_a...  61.4 us
    dot_general x2, matrix products, term_maker(): lax.dot_general(sq_acts, sq_grads, (((0,), (0,)), ((), ())), preferred_el...  54.6 us
    gather x6, local copies, waits for them, and re-layouts, unpack_blocks(): picked = jnp.take(received, recv_slot, axis=1)  41 us
    scatter x2, local copies, waits for them, and re-layouts, pack_blocks(): return empty.at[:, send_slot, :].set(split)  25.8 us
  transfers between devices with their start and end apart: 4, of which 3 were waited for; matrix products, arithmetic and copies ran while one was open for 11% of the time, Pallas kernels for 0%

commit v1 on v0

v1 whole, which is shorter than its diff:
```python
import jax
import jax.numpy as jnp
from jax import lax
from jax.sharding import PartitionSpec as P

BLK = 128
CORES = 2
EPSILON = 1e-06


def squared(values):
    wide = values.astype(jnp.float32)
    return (wide * wide).astype(jnp.bfloat16)


def block_plan(block_match, me, per_dev, capacity, slots):
    total = block_match.shape[0]
    place = jnp.arange(total, dtype=jnp.int32)
    target_dev = place // per_dev
    source_dev = block_match // per_dev
    earlier = (
        (source_dev[:, None] == source_dev[None, :])
        & (target_dev[:, None] == target_dev[None, :])
        & (place[None, :] < place[:, None])
    )
    rank = jnp.sum(earlier.astype(jnp.int32), axis=1)
    out_slot = jnp.where(source_dev == me, target_dev * capacity + rank, -1)
    hits = out_slot[None, :] == jnp.arange(slots, dtype=jnp.int32)[:, None]
    send_block = jnp.sum(jnp.where(hits, (block_match % per_dev)[None, :], 0), axis=1)
    recv_slot = lax.dynamic_slice_in_dim(source_dev * capacity + rank, me * per_dev, per_dev)
    return send_block, recv_slot


def take_blocks(data, ids):
    rows = data.shape[0]
    pieces = [
        lax.dynamic_slice(data, (0, ids[j] * BLK), (rows, BLK)) for j in range(ids.shape[0])
    ]
    return jnp.concatenate(pieces, axis=1)


def match_blocks(data, block_match):
    neurons = lax.axis_size("neuron")
    me = lax.axis_index("neuron")
    per_dev = data.shape[1] // BLK
    capacity = (per_dev + neurons - 1) // neurons
    send_block, recv_slot = block_plan(block_match, me, per_dev, capacity, neurons * capacity)
    rows = data.shape[0]
    width = capacity * BLK
    got = []
    for shift in range(neurons):
        target = (me + shift) % neurons
        ids = lax.dynamic_slice_in_dim(send_block, target * capacity, capacity)
        piece = take_blocks(data, ids)
        if shift:
            piece = lax.ppermute(
                piece, "neuron", [(i, (i + shift) % neurons) for i in range(neurons)]
            )
        got.append(piece)
    received = jnp.concatenate(got, axis=1)
    source = recv_slot // capacity
    place = ((me - source) % neurons) * capacity + recv_slot % capacity
    return take_blocks(received, place)


def gather_acts(acts, chips, inward):
    neurons = lax.axis_size("neuron")
    n_me = lax.axis_index("neuron")
    me = lax.axis_index("dp")
    z, core = me // CORES, me % CORES
    share = acts.shape[0] // neurons
    mine = squared(lax.dynamic_slice_in_dim(acts, n_me * share, share, axis=0)).T
    mine = lax.all_to_all(mine, "dp", split_axis=0, concat_axis=1, tiled=True)
    end = lax.ppermute(mine, "dp", inward)
    both = jnp.concatenate([mine, end], axis=0)
    whole = lax.all_gather(both, "neuron", axis=0)
    sides = []
    for side in range(CORES):
        who = (core + side) % CORES
        groups = []
        for s in range(chips):
            start = (((z - s) % chips) * CORES + who) * share
            groups += [
                lax.dynamic_slice(whole, (n, 0, start), (1, both.shape[0], share))[0]
                for n in range(neurons)
            ]
        sides.append(jnp.concatenate(groups, axis=1))
    return sides


def after(values, *earlier):
    return lax.optimization_barrier((values, *earlier))[0]


def z_pairs(pairs):
    return [(a * CORES + c, b * CORES + c) for a, b in pairs for c in range(CORES)]


def on_device(acts_a, acts_b, grads_a, grads_b, weights_a, weights_b, block_match):
    dp = lax.axis_size("dp")
    chips = dp // CORES
    me = lax.axis_index("dp")
    z = me // CORES
    is_end = (z == 0) | (z == chips - 1)
    rows = weights_a.shape[0]
    tokens = grads_a.shape[0]
    per_dev = grads_a.shape[1] // BLK
    pieces = max(n for n in range(1, 5) if per_dev % n == 0)
    width = grads_a.shape[1] // pieces
    inward = z_pairs([(0, 1), (chips - 1, chips - 2)])
    outward = z_pairs([(1, 0), (chips - 2, chips - 1)])
    swap = [(i, i + 1 - 2 * (i % CORES)) for i in range(dp)]

    def spread(block, inner):
        up, down = block, block
        ups, downs = {}, {}
        skip = 1 if inner else 0
        for hop in range(1, chips - skip):
            up = lax.ppermute(
                up, "dp", z_pairs([(i, i + 1) for i in range(hop - 1, chips - 1 - skip)])
            )
            down = lax.ppermute(
                down, "dp", z_pairs([(i, i - 1) for i in range(1 + skip, chips - hop + 1)])
            )
            ups[hop], downs[hop] = up, down
        slots = [block]
        for s in range(1, chips):
            if s in ups and chips - s in downs:
                slots.append(jnp.where(z >= s, ups[s], downs[chips - s]))
            elif s in ups:
                slots.append(ups[s])
            else:
                slots.append(downs[chips - s])
        held = jnp.concatenate(slots, axis=0)
        return held, lax.ppermute(held, "dp", swap)

    def multiply(sides, pair):
        return sum(
            jnp.dot(side, block, preferred_element_type=jnp.float32)
            for side, block in zip(sides, pair)
        )

    def cut(values, p):
        return values[:, p * width : (p + 1) * width]

    sq_a = squared(grads_a)
    sides = gather_acts(acts_a, chips, inward)
    blocks = [cut(sq_a, p) for p in range(pieces)]
    fishers, totals, sums = [], [], []
    for p in range(2 * pieces):
        block = blocks[p]
        if p >= 2:
            block = after(block, totals[p - 2], *sums[max(p - 3, 0) : p - 2])
        if p == pieces:
            sides = sides_b
        pair = spread(block, p > 0)
        if p == 0:
            total = multiply([side[:rows] for side in sides], pair)
            fishers.append(total)
            sums.append(total)
            totals.append(total)
            late = after((grads_b, weights_b, acts_b), total)
            both_b = jnp.concatenate([squared(late[0]), late[1]], axis=0)
            moved = match_blocks(both_b, block_match)
            sq_b, weights_match = moved[:tokens], moved[tokens:]
            sides_b = gather_acts(late[2], chips, inward)
            blocks += [cut(sq_b, q) for q in range(pieces)]
            continue
        total = multiply(sides, pair)
        totals.append(total)
        sums.append(lax.ppermute(total[rows:], "dp", outward))
        fishers.append(jnp.where(is_end, sums[-1], total[:rows]))
    merged = []
    for p in range(pieces):
        fisher_a, fisher_b = fishers[p], fishers[pieces + p]
        wide_a = cut(weights_a, p).astype(jnp.float32)
        wide_b = cut(weights_match, p).astype(jnp.float32)
        merged.append(
            (fisher_a * wide_a + fisher_b * wide_b) / (fisher_a + fisher_b + EPSILON)
        )
    return jnp.concatenate(merged, axis=1)


def solution(mesh):
    placed = (
        P("dp", None),
        P("dp", None),
        P("dp", "neuron"),
        P("dp", "neuron"),
        P("dp", "neuron"),
        P("dp", "neuron"),
        P(),
    )
    return jax.shard_map(
        on_device, mesh=mesh, in_specs=placed, out_specs=P("dp", "neuron"), check_vma=False
    )
```

time: 1180 us -> 899 us (0.76)
  waiting for transfers between devices: 986 us -> 356 us
  starting transfers between devices: 10.6 us -> 135 us
  other arithmetic: 12.4 us -> 118 us
  matrix products: 54.6 us -> 111 us
  between operations: 13.5 us -> 50.6 us
  blocking collectives: 0 us -> 32.7 us
  local copies, waits for them, and re-layouts: 103 us -> 87 us
    reduce_scatter x2 -> x0, waiting for transfers between devices: 924 us -> none  [the longest x1 506 us: on_device(): lax.psum_scatter(term_maker(sq_acts_b, sq_grads_b), 'dp', scatter_dimensi...]
    ppermute x0 -> x54, waiting for transfers between devices: none -> 347 us  [the longest x7 143 us: on_device(): sums.append(lax.ppermute(total[rows:], 'dp', outward))]
    ppermute x0 -> x54, starting transfers between devices: none -> 131 us  [the longest x17 90.7 us: spread(): lax.ppermute(up, 'dp', z_pairs([(i, i + 1) for i in range(hop - 1, chips...]
    concatenate x0 -> x14, other arithmetic: none -> 72.8 us  [the longest x8 63.1 us: spread(): held = jnp.concatenate(slots, axis=0)]
    dot_general x2 -> x16, matrix products: 54.6 us -> 111 us  [multiply(): jnp.dot(side, block, preferred_element_type=jnp.float32)]
    all_to_all x2 -> x1, waiting for transfers between devices: 61.4 us -> 8.69 us  [gather_acts(): mine = lax.all_to_all(mine, 'dp', split_axis=0, concat_axis=1, tiled=True)]
    gather x7 -> x0, local copies, waits for them, and re-layouts: 41.7 us -> none  [the longest x6 41 us: unpack_blocks(): picked = jnp.take(received, recv_slot, axis=1)]
    unnamed x3 -> x157, local copies, waits for them, and re-layouts: 5.98 us -> 40 us
  transfers between devices with their start and end apart: 4 -> 57, of which waited for: 3 -> 17; matrix products, arithmetic and copies ran while one was open for 11% -> 32% of each run, Pallas kernels for 0% -> 0%
where the time goes in v1:
time: 899 us; the launch traced here: 890 us
  waiting for transfers between devices  356 us (40%)
  starting transfers between devices  135 us (15%)
  other arithmetic  118 us (13%)
  matrix products  111 us (12%)
  local copies, waits for them, and re-layouts  87 us (10%)
  between operations  50.6 us (6%)
  blocking collectives  32.7 us (4%)
    ppermute x7, waiting for transfers between devices, on_device(): sums.append(lax.ppermute(total[rows:], 'dp', outward))  143 us
    dot_general x16, matrix products, multiply(): jnp.dot(side, block, preferred_element_type=jnp.float32)  111 us
    ppermute x17, starting transfers between devices, spread(): lax.ppermute(up, 'dp', z_pairs([(i, i + 1) for i in range(hop - 1, chips...  90.7 us
    ppermute x3, waiting for transfers between devices, match_blocks(): lax.ppermute(piece, 'neuron', [(i, (i + shift) % neurons) for i in range(...  68.6 us
    concatenate x8, other arithmetic, spread(): held = jnp.concatenate(slots, axis=0)  63.1 us
    ppermute x17, waiting for transfers between devices, spread(): lax.ppermute(up, 'dp', z_pairs([(i, i + 1) for i in range(hop - 1, chips...  55.2 us
    ppermute x2, waiting for transfers between devices, gather_acts(): end = lax.ppermute(mine, 'dp', inward)  48.4 us
    unnamed x157, local copies, waits for them, and re-layouts  40 us
  transfers between devices with their start and end apart: 57, of which 17 were waited for; matrix products, arithmetic and copies ran while one was open for 32% of the time, Pallas kernels for 0%

profile of v1, /device:TPU:0, one launch (start us, length us, event | category | flops | bytes accessed | tf_op | source)
XLA Modules:
  0.0 889.8 jit_solution(12672288636024047296)
XLA Ops:
  8.7 32.7 %all_to_all.38 = bf16[8,512,128]{2,1,0:T(8,128)(2,1)S(1)} all-to-all(bf16[8,512,128]{2,1,0:T(8,128)(2,1)S(1)} %bitcast.251), channel_id=1, replica_groups=mesh['dp'=8,'neuron'=4] {'dp'}, dimensions={0} | all-to-all | bytes 2097152 | tf_op jit(solution)/shard_map/all_to_all | solution.py:73
  43.6 22.0 %collective-permute-done = bf16[512,1024]{0,1:T(8,128)(2,1)S(1)} collective-permute-done((bf16[512,1024]{0,1:T(8,128)(2,1)S(1)}, bf16[512,1024]{0,1:T(8,128)(2,1)S(1)}, u32[]{:S(2)}, u32[]{:S(2)}) %collective-permute-start) | collective-permute-done | bytes 1048608 | tf_op jit(solution)/shard_map/ppermute | solution.py:74
  76.9 17.0 %collective-permute-done.1 = bf16[512,896]{1,0:T(8,128)(2,1)S(1)} collective-permute-done((bf16[512,896]{1,0:T(8,128)(2,1)S(1)}, bf16[512,896]{1,0:T(8,128)(2,1)S(1)}, u32[]{:S(2)}, u32[]{:S(2)}) %collective-permute-start.1) | collective-permute-done | bytes 917536 | tf_op jit(solution)/shard_map/ppermute | solution.py:119
  101.0 20.1 %collective-permute-done.3 = bf16[512,896]{1,0:T(8,128)(2,1)} collective-permute-done((bf16[512,896]{1,0:T(8,128)(2,1)S(1)}, bf16[512,896]{1,0:T(8,128)(2,1)}, u32[]{:S(2)}, u32[]{:S(2)}) %collective-permute-start.3) | collective-permute-done | bytes 917536 | tf_op jit(solution)/shard_map/ppermute | solution.py:122
  124.0 6.2 collective-permute-start.17
  133.2 9.7 %collective-permute-done.4 = bf16[512,896]{1,0:T(8,128)(2,1)} collective-permute-done((bf16[512,896]{1,0:T(8,128)(2,1)}, bf16[512,896]{1,0:T(8,128)(2,1)}, u32[]{:S(2)}, u32[]{:S(2)}) %collective-permute-start.4) | collective-permute-done | bytes 917536 | tf_op jit(solution)/shard_map/ppermute | solution.py:122
  144.2 8.7 pad_maximum_fusion.1
  176.9 7.7 pad_maximum_fusion.3
  185.1 12.0 %copy.214 = bf16[4096,1024]{1,0:T(8,128)(2,1)} copy(bf16[4096,1024]{0,1:T(8,128)(2,1)} %all-gather.5.cloned.1.call-done) | data formatting | bytes 16777216 | tf_op jit(solution)/shard_map/all_gather | solution.py:76
  209.5 7.2 fusion
  221.9 6.0 collective-permute-start.12
  227.9 6.4 copy.152
  240.7 7.5 fusion.76
  248.3 7.9 convolution_add_fusion.5
  262.2 8.7 all-to-all-done.1
  280.0 26.4 %collective-permute-done.8 = bf16[512,1024]{0,1:T(8,128)(2,1)S(1)} collective-permute-done((bf16[512,1024]{0,1:T(8,128)(2,1)S(1)}, bf16[512,1024]{0,1:T(8,128)(2,1)S(1)}, u32[]{:S(2)}, u32[]{:S(2)}) %collective-permute-start.8) | collective-permute-done | bytes 1048608 | tf_op jit(solution)/shard_map/ppermute | solution.py:74
  325.2 7.7 pad_maximum_fusion.2
  369.2 6.6 pad_maximum_fusion.5
  378.1 4.8 collective-permute-done.9
  384.5 63.8 %collective-permute-done.10 = bf16[1024,896]{1,0:T(8,128)(2,1)} collective-permute-done((bf16[1024,896]{1,0:T(8,128)(2,1)}, bf16[1024,896]{1,0:T(8,128)(2,1)}, u32[]{:S(2)}, u32[]{:S(2)}) %collective-permute-start.10) | collective-permute-done | bytes 1835040 | tf_op jit(solution)/shard_map/ppermute | solution.py:56
  457.0 10.3 %fusion.75 = f32[1024,896]{1,0:T(8,128)} fusion(bf16[1024,2048]{1,0:T(8,128)(2,1)S(1)} %copy-done.57, bf16[2048,896]{1,0:T(8,128)(2,1)} %collective-permute-done.16), kind=kOutput, calls=%fused_computation.285 | convolution fusion | flops 3758096384 | bytes 11534336 | tf_op jit(solution)/shard_map/dot_general | solution.py:139
  467.3 7.4 convolution_add_fusion.6
  475.5 30.7 %collective-permute-start.23 = (bf16[512,896]{1,0:T(8,128)(2,1)S(1)}, bf16[512,896]{1,0:T(8,128)(2,1)S(1)}, u32[]{:S(2)}, u32[]{:S(2)}) collective-permute-start(bf16[512,896]{1,0:T(8,128)(2,1)S(1)} %slice.373), channel_id=1, source_target_pairs={{0,8},{4,12},{8,16},{12,20},{1,9},{5,13},{9,17},{13,21},{2,10},{6,... | collective-permute-start | bytes 2752520 | tf_op jit(solution)/shard_map/ppermute | solution.py:119
  508.3 9.6 %fusion.78 = f32[1024,896]{1,0:T(8,128)} fusion(bf16[1024,2048]{1,0:T(8,128)(2,1)} %copy-done.56, bf16[2048,896]{1,0:T(8,128)(2,1)} %collective-permute-done.33), kind=kOutput, calls=%fused_computation.288 | convolution fusion | flops 3758096384 | bytes 11534336 | tf_op jit(solution)/shard_map/dot_general | solution.py:139
  518.0 7.9 collective-permute-done.23
  527.3 7.1 convolution_add_fusion.3
  534.4 15.8 %collective-permute-done.34 = f32[512,896]{1,0:T(8,128)S(1)} collective-permute-done((f32[512,896]{1,0:T(8,128)S(1)}, f32[512,896]{1,0:T(8,128)S(1)}, u32[]{:S(2)}, u32[]{:S(2)}) %collective-permute-start.34) | collective-permute-done | bytes 1835040 | tf_op jit(solution)/shard_map/ppermute | solution.py:171
  552.6 8.7 pad_maximum_fusion.4
  561.3 8.9 %collective-permute-done.35 = bf16[512,896]{1,0:T(8,128)(2,1)S(1)} collective-permute-done((bf16[512,896]{1,0:T(8,128)(2,1)S(1)}, bf16[512,896]{1,0:T(8,128)(2,1)S(1)}, u32[]{:S(2)}, u32[]{:S(2)}) %collective-permute-start.35) | collective-permute-done | bytes 917536 | tf_op jit(solution)/shard_map/ppermute | solution.py:119
  575.8 8.6 pad_maximum_fusion.6
  584.5 12.0 %copy.215 = bf16[4096,1024]{1,0:T(8,128)(2,1)} copy(bf16[4096,1024]{0,1:T(8,128)(2,1)} %all-gather.7.cloned.1.call-done) | data formatting | bytes 16777216 | tf_op jit(solution)/shard_map/all_gather | solution.py:76
  609.0 6.7 fusion.77
  615.7 4.5 convolution_add_fusion.4
  621.2 25.5 %collective-permute-start.42 = (bf16[512,896]{1,0:T(8,128)(2,1)S(1)}, bf16[512,896]{1,0:T(8,128)(2,1)S(1)}, u32[]{:S(2)}, u32[]{:S(2)}) collective-permute-start(bf16[512,896]{1,0:T(8,128)(2,1)S(1)} %slice.388), channel_id=1, source_target_pairs={{0,8},{4,12},{8,16},{12,20},{1,9},{5,13},{9,17},{13,21},{2,10},{6,... | collective-permute-start | bytes 2752520 | tf_op jit(solution)/shard_map/ppermute | solution.py:119
  648.4 8.4 fusion.79
  656.9 10.1 %collective-permute-done.42 = bf16[512,896]{1,0:T(8,128)(2,1)S(1)} collective-permute-done((bf16[512,896]{1,0:T(8,128)(2,1)S(1)}, bf16[512,896]{1,0:T(8,128)(2,1)S(1)}, u32[]{:S(2)}, u32[]{:S(2)}) %collective-permute-start.42) | collective-permute-done | bytes 917536 | tf_op jit(solution)/shard_map/ppermute | solution.py:119
  668.4 6.6 convolution_add_fusion.2
  675.0 15.8 %collective-permute-done.28 = f32[512,896]{1,0:T(8,128)S(1)} collective-permute-done((f32[512,896]{1,0:T(8,128)S(1)}, f32[512,896]{1,0:T(8,128)S(1)}, u32[]{:S(2)}, u32[]{:S(2)}) %collective-permute-start.28) | collective-permute-done | bytes 1835040 | tf_op jit(solution)/shard_map/ppermute | solution.py:171
  693.7 7.5 pad_maximum_fusion.7
  701.3 11.3 %collective-permute-done.48 = bf16[512,896]{1,0:T(8,128)(2,1)S(1)} collective-permute-done((bf16[512,896]{1,0:T(8,128)(2,1)S(1)}, bf16[512,896]{1,0:T(8,128)(2,1)S(1)}, u32[]{:S(2)}, u32[]{:S(2)}) %collective-permute-start.48) | collective-permute-done | bytes 917536 | tf_op jit(solution)/shard_map/ppermute | solution.py:119
  714.4 7.5 pad_maximum_fusion.8
  724.6 6.4 fusion.80
  731.0 6.6 convolution_add_fusion.1
  740.7 6.5 fusion.81
  747.2 4.5 convolution_add_fusion
  756.2 76.0 %collective-permute-done.47 = f32[512,896]{1,0:T(8,128)} collective-permute-done((f32[512,896]{1,0:T(8,128)}, f32[512,896]{1,0:T(8,128)}, u32[]{:S(2)}, u32[]{:S(2)}) %collective-permute-start.47) | collective-permute-done | bytes 1835040 | tf_op jit(solution)/shard_map/ppermute | solution.py:171
  836.3 35.1 %collective-permute-done.53 = f32[512,896]{1,0:T(8,128)} collective-permute-done((f32[512,896]{1,0:T(8,128)}, f32[512,896]{1,0:T(8,128)}, u32[]{:S(2)}, u32[]{:S(2)}) %collective-permute-start.53) | collective-permute-done | bytes 1835040 | tf_op jit(solution)/shard_map/ppermute | solution.py:171
  871.4 7.8 add_divide_fusion.3
  (325 shorter events, 176.3 us)
Async XLA Ops:
  6.5 178.6 %all-gather.5.cloned.1.call-start = ((), (), s32[]{:S(2)}) async-start(), calls=%async_computation.2 | async-start | bytes 10485760 | tf_op jit(solution)/shard_map/all_gather | solution.py:76
  42.0 23.6 %collective-permute-start = (bf16[512,1024]{0,1:T(8,128)(2,1)S(1)}, bf16[512,1024]{0,1:T(8,128)(2,1)S(1)}, u32[]{:S(2)}, u32[]{:S(2)}) collective-permute-start(bf16[512,1024]{0,1:T(8,128)(2,1)S(1)} %bitcast.255), channel_id=1, source_target_pairs={{0,8},{4,12},{24,16},{28,20},{1,9},{5,13},{25,17},{29,21},{2,10},{... | collective-permute-start | bytes 3145736 | tf_op jit(solution)/shard_map/ppermute | solution.py:74
  71.2 22.7 %collective-permute-start.1 = (bf16[512,896]{1,0:T(8,128)(2,1)S(1)}, bf16[512,896]{1,0:T(8,128)(2,1)S(1)}, u32[]{:S(2)}, u32[]{:S(2)}) collective-permute-start(bf16[512,896]{1,0:T(8,128)(2,1)S(1)} %get-tuple-element.130), channel_id=1, source_target_pairs={{0,8},{4,12},{8,16},{12,20},{16,24},{20,28},{1,9},{5,13},{9,17},{1... | collective-permute-start | bytes 2752520 | tf_op jit(solution)/shard_map/ppermute | solution.py:119
  75.6 22.5 %collective-permute-start.2 = (bf16[512,896]{1,0:T(8,128)(2,1)S(1)}, bf16[512,896]{1,0:T(8,128)(2,1)S(1)}, u32[]{:S(2)}, u32[]{:S(2)}) collective-permute-start(bf16[512,896]{1,0:T(8,128)(2,1)S(1)} %get-tuple-element.130), channel_id=1, source_target_pairs={{8,0},{12,4},{16,8},{20,12},{24,16},{28,20},{9,1},{13,5},{17,9},{2... | collective-permute-start | bytes 2752520 | tf_op jit(solution)/shard_map/ppermute | solution.py:122
  98.0 23.0 %collective-permute-start.3 = (bf16[512,896]{1,0:T(8,128)(2,1)S(1)}, bf16[512,896]{1,0:T(8,128)(2,1)}, u32[]{:S(2)}, u32[]{:S(2)}) collective-permute-start(bf16[512,896]{1,0:T(8,128)(2,1)S(1)} %collective-permute-done.2), channel_id=1, source_target_pairs={{8,0},{12,4},{16,8},{20,12},{9,1},{13,5},{17,9},{21,13},{10,2},{14... | collective-permute-start | bytes 2752520 | tf_op jit(solution)/shard_map/ppermute | solution.py:122
  99.3 32.2 %collective-permute-start.6 = (bf16[512,896]{1,0:T(8,128)(2,1)}, bf16[512,896]{1,0:T(8,128)(2,1)}, u32[]{:S(2)}, u32[]{:S(2)}) collective-permute-start(bf16[512,896]{1,0:T(8,128)(2,1)} %collective-permute-done.5), channel_id=1, source_target_pairs={{16,24},{20,28},{17,25},{21,29},{18,26},{22,30},{19,27},{23,31}} | collective-permute-start | bytes 2752520 | tf_op jit(solution)/shard_map/ppermute | solution.py:119
  121.1 21.8 %collective-permute-start.4 = (bf16[512,896]{1,0:T(8,128)(2,1)}, bf16[512,896]{1,0:T(8,128)(2,1)}, u32[]{:S(2)}, u32[]{:S(2)}) collective-permute-start(bf16[512,896]{1,0:T(8,128)(2,1)} %collective-permute-done.3), channel_id=1, source_target_pairs={{8,0},{12,4},{9,1},{13,5},{10,2},{14,6},{11,3},{15,7}} | collective-permute-start | bytes 2752520 | tf_op jit(solution)/shard_map/ppermute | solution.py:122
  122.4 32.2 %collective-permute-start.19 = (bf16[512,896]{1,0:T(8,128)(2,1)S(1)}, bf16[512,896]{1,0:T(8,128)(2,1)}, u32[]{:S(2)}, u32[]{:S(2)}) collective-permute-start(bf16[512,896]{1,0:T(8,128)(2,1)S(1)} %get-tuple-element.129), channel_id=1, source_target_pairs={{16,8},{20,12},{24,16},{28,20},{17,9},{21,13},{25,17},{29,21},{18,... | collective-permute-start | bytes 2752520 | tf_op jit(solution)/shard_map/ppermute | solution.py:122
  124.0 29.0 %collective-permute-start.17 = (bf16[512,896]{1,0:T(8,128)(2,1)S(1)}, bf16[512,896]{1,0:T(8,128)(2,1)}, u32[]{:S(2)}, u32[]{:S(2)}) collective-permute-start(bf16[512,896]{1,0:T(8,128)(2,1)S(1)} %get-tuple-element.129), channel_id=1, source_target_pairs={{0,8},{4,12},{8,16},{12,20},{1,9},{5,13},{9,17},{13,21},{2,10},{6,... | collective-permute-start | bytes 2752520 | tf_op jit(solution)/shard_map/ppermute | solution.py:119
  152.9 56.5 %collective-permute-start.7 = (bf16[2048,896]{1,0:T(8,128)(2,1)}, bf16[2048,896]{1,0:T(8,128)(2,1)}, u32[]{:S(2)}, u32[]{:S(2)}) collective-permute-start(bf16[2048,896]{1,0:T(8,128)(2,1)} %pad_maximum_fusion.1), channel_id=1, source_target_pairs={{0,4},{4,0},{8,12},{12,8},{16,20},{20,16},{24,28},{28,24},{1,5},{5... | collective-permute-start | bytes 11010056 | tf_op jit(solution)/shard_map/ppermute | solution.py:135
  153.0 21.7 %collective-permute-start.18 = (bf16[512,896]{1,0:T(8,128)(2,1)}, bf16[512,896]{1,0:T(8,128)(2,1)}, u32[]{:S(2)}, u32[]{:S(2)}) collective-permute-start(bf16[512,896]{1,0:T(8,128)(2,1)} %collective-permute-done.17), channel_id=1, source_target_pairs={{8,16},{12,20},{9,17},{13,21},{10,18},{14,22},{11,19},{15,23}} | collective-permute-start | bytes 2752520 | tf_op jit(solution)/shard_map/ppermute | solution.py:119
  154.6 20.1 %collective-permute-start.20 = (bf16[512,896]{1,0:T(8,128)(2,1)}, bf16[512,896]{1,0:T(8,128)(2,1)}, u32[]{:S(2)}, u32[]{:S(2)}) collective-permute-start(bf16[512,896]{1,0:T(8,128)(2,1)} %collective-permute-done.19), channel_id=1, source_target_pairs={{16,8},{20,12},{17,9},{21,13},{18,10},{22,14},{19,11},{23,15}} | collective-permute-start | bytes 2752520 | tf_op jit(solution)/shard_map/ppermute | solution.py:122
  184.6 56.1 %collective-permute-start.21 = (bf16[2048,896]{1,0:T(8,128)(2,1)}, bf16[2048,896]{1,0:T(8,128)(2,1)}, u32[]{:S(2)}, u32[]{:S(2)}) collective-permute-start(bf16[2048,896]{1,0:T(8,128)(2,1)} %pad_maximum_fusion.3), channel_id=1, source_target_pairs={{0,4},{4,0},{8,12},{12,8},{16,20},{20,16},{24,28},{28,24},{1,5},{5... | collective-permute-start | bytes 11010056 | tf_op jit(solution)/shard_map/ppermute | solution.py:135
  220.3 95.7 %collective-permute-start.14 = (bf16[512,896]{1,0:T(8,128)(2,1)}, bf16[512,896]{1,0:T(8,128)(2,1)}, u32[]{:S(2)}, u32[]{:S(2)}) collective-permute-start(bf16[512,896]{1,0:T(8,128)(2,1)} %get-tuple-element.17), channel_id=1, source_target_pairs={{16,8},{20,12},{24,16},{28,20},{17,9},{21,13},{25,17},{29,21},{18,... | collective-permute-start | bytes 2752520 | tf_op jit(solution)/shard_map/ppermute | solution.py:122
  221.9 93.4 %collective-permute-start.12 = (bf16[512,896]{1,0:T(8,128)(2,1)}, bf16[512,896]{1,0:T(8,128)(2,1)}, u32[]{:S(2)}, u32[]{:S(2)}) collective-permute-start(bf16[512,896]{1,0:T(8,128)(2,1)} %get-tuple-element.17), channel_id=1, source_target_pairs={{0,8},{4,12},{8,16},{12,20},{1,9},{5,13},{9,17},{13,21},{2,10},{6,... | collective-permute-start | bytes 2752520 | tf_op jit(solution)/shard_map/ppermute | solution.py:119
  236.7 34.2 %all-to-all-start.1 = ((bf16[8,512,128]{2,1,0:T(8,128)(2,1)}), bf16[8,512,128]{2,1,0:T(8,128)(2,1)S(1)}, u32[]{:S(2)}, u32[]{:S(2)}) async-start(bf16[8,512,128]{2,1,0:T(8,128)(2,1)} %bitcast.37), calls=%async_computation.1 | async-start | bytes 2097152 | tf_op jit(solution)/shard_map/all_to_all | solution.py:73
  240.3 344.2 %all-gather.7.cloned.1.call-start = ((), (), s32[]{:S(2)}) async-start(), calls=%async_computation.3 | async-start | bytes 10485760 | tf_op jit(solution)/shard_map/all_gather | solution.py:76
  256.1 81.4 %collective-permute-start.31 = (bf16[512,896]{1,0:T(8,128)(2,1)S(1)}, bf16[512,896]{1,0:T(8,128)(2,1)}, u32[]{:S(2)}, u32[]{:S(2)}) collective-permute-start(bf16[512,896]{1,0:T(8,128)(2,1)S(1)} %get-tuple-element.19), channel_id=1, source_target_pairs={{16,8},{20,12},{24,16},{28,20},{17,9},{21,13},{25,17},{29,21},{18,... | collective-permute-start | bytes 2752520 | tf_op jit(solution)/shard_map/ppermute | solution.py:122
  257.7 65.7 %collective-permute-start.29 = (bf16[512,896]{1,0:T(8,128)(2,1)S(1)}, bf16[512,896]{1,0:T(8,128)(2,1)}, u32[]{:S(2)}, u32[]{:S(2)}) collective-permute-start(bf16[512,896]{1,0:T(8,128)(2,1)S(1)} %get-tuple-element.19), channel_id=1, source_target_pairs={{0,8},{4,12},{8,16},{12,20},{1,9},{5,13},{9,17},{13,21},{2,10},{6,... | collective-permute-start | bytes 2752520 | tf_op jit(solution)/shard_map/ppermute | solution.py:119
  271.4 35.1 %collective-permute-start.8 = (bf16[512,1024]{0,1:T(8,128)(2,1)S(1)}, bf16[512,1024]{0,1:T(8,128)(2,1)S(1)}, u32[]{:S(2)}, u32[]{:S(2)}) collective-permute-start(bf16[512,1024]{0,1:T(8,128)(2,1)S(1)} %bitcast.253), channel_id=1, source_target_pairs={{0,8},{4,12},{24,16},{28,20},{1,9},{5,13},{25,17},{29,21},{2,10},{... | collective-permute-start | bytes 3145736 | tf_op jit(solution)/shard_map/ppermute | solution.py:74
  332.9 121.9 %collective-permute-start.16 = (bf16[2048,896]{1,0:T(8,128)(2,1)}, bf16[2048,896]{1,0:T(8,128)(2,1)}, u32[]{:S(2)}, u32[]{:S(2)}) collective-permute-start(bf16[2048,896]{1,0:T(8,128)(2,1)} %pad_maximum_fusion.2), channel_id=1, source_target_pairs={{0,4},{4,0},{8,12},{12,8},{16,20},{20,16},{24,28},{28,24},{1,5},{5... | collective-permute-start | bytes 11010056 | tf_op jit(solution)/shard_map/ppermute | solution.py:135
  336.0 46.9 %collective-permute-start.9 = (bf16[1024,896]{1,0:T(8,128)(2,1)}, bf16[1024,896]{1,0:T(8,128)(2,1)S(1)}, u32[]{:S(2)}, u32[]{:S(2)}) collective-permute-start(bf16[1024,896]{1,0:T(8,128)(2,1)} %get-tuple-element.122), channel_id=1, source_target_pairs={{0,1},{1,2},{2,3},{3,0},{4,5},{5,6},{6,7},{7,4},{8,9},{9,10},{10,1... | collective-permute-start | bytes 5505032 | tf_op jit(solution)/shard_map/ppermute | solution.py:56
  337.6 30.4 %collective-permute-start.32 = (bf16[512,896]{1,0:T(8,128)(2,1)}, bf16[512,896]{1,0:T(8,128)(2,1)}, u32[]{:S(2)}, u32[]{:S(2)}) collective-permute-start(bf16[512,896]{1,0:T(8,128)(2,1)} %collective-permute-done.31), channel_id=1, source_target_pairs={{16,8},{20,12},{17,9},{21,13},{18,10},{22,14},{19,11},{23,15}} | collective-permute-start | bytes 2752520 | tf_op jit(solution)/shard_map/ppermute | solution.py:122
  339.2 109.1 %collective-permute-start.10 = (bf16[1024,896]{1,0:T(8,128)(2,1)}, bf16[1024,896]{1,0:T(8,128)(2,1)}, u32[]{:S(2)}, u32[]{:S(2)}) collective-permute-start(bf16[1024,896]{1,0:T(8,128)(2,1)} %get-tuple-element.119), channel_id=1, source_target_pairs={{0,2},{1,3},{2,0},{3,1},{4,6},{5,7},{6,4},{7,5},{8,10},{9,11},{10,... | collective-permute-start | bytes 5505032 | tf_op jit(solution)/shard_map/ppermute | solution.py:56
  340.7 109.4 %collective-permute-start.11 = (bf16[1024,896]{1,0:T(8,128)(2,1)}, bf16[1024,896]{1,0:T(8,128)(2,1)}, u32[]{:S(2)}, u32[]{:S(2)}) collective-permute-start(bf16[1024,896]{1,0:T(8,128)(2,1)} %get-tuple-element.115), channel_id=1, source_target_pairs={{0,3},{1,0},{2,1},{3,2},{4,7},{5,4},{6,5},{7,6},{8,11},{9,8},{10,9... | collective-permute-start | bytes 5505032 | tf_op jit(solution)/shard_map/ppermute | solution.py:56
  375.9 132.4 %collective-permute-start.33 = (bf16[2048,896]{1,0:T(8,128)(2,1)S(1)}, bf16[2048,896]{1,0:T(8,128)(2,1)}, u32[]{:S(2)}, u32[]{:S(2)}) collective-permute-start(bf16[2048,896]{1,0:T(8,128)(2,1)S(1)} %pad_maximum_fusion.5), channel_id=1, source_target_pairs={{0,4},{4,0},{8,12},{12,8},{16,20},{20,16},{24,28},{28,24},{1,5},{5... | collective-permute-start | bytes 11010056 | tf_op jit(solution)/shard_map/ppermute | solution.py:135
  382.9 91.8 %collective-permute-start.22 = (f32[512,896]{1,0:T(8,128)S(1)}, f32[512,896]{1,0:T(8,128)S(1)}, u32[]{:S(2)}, u32[]{:S(2)}) collective-permute-start(f32[512,896]{1,0:T(8,128)S(1)} %slice.376), channel_id=1, source_target_pairs={{8,0},{12,4},{16,24},{20,28},{9,1},{13,5},{17,25},{21,29},{10,2},{... | collective-permute-start | bytes 5505032 | tf_op jit(solution)/shard_map/ppermute | solution.py:171
  474.8 51.8 %collective-permute-start.25 = (bf16[512,896]{1,0:T(8,128)(2,1)S(1)}, bf16[512,896]{1,0:T(8,128)(2,1)S(1)}, u32[]{:S(2)}, u32[]{:S(2)}) collective-permute-start(bf16[512,896]{1,0:T(8,128)(2,1)S(1)} %slice.373), channel_id=1, source_target_pairs={{16,8},{20,12},{24,16},{28,20},{17,9},{21,13},{25,17},{29,21},{18,... | collective-permute-start | bytes 2752520 | tf_op jit(solution)/shard_map/ppermute | solution.py:122
  475.5 50.3 %collective-permute-start.23 = (bf16[512,896]{1,0:T(8,128)(2,1)S(1)}, bf16[512,896]{1,0:T(8,128)(2,1)S(1)}, u32[]{:S(2)}, u32[]{:S(2)}) collective-permute-start(bf16[512,896]{1,0:T(8,128)(2,1)S(1)} %slice.373), channel_id=1, source_target_pairs={{0,8},{4,12},{8,16},{12,20},{1,9},{5,13},{9,17},{13,21},{2,10},{6,... | collective-permute-start | bytes 2752520 | tf_op jit(solution)/shard_map/ppermute | solution.py:119
  506.3 43.8 %collective-permute-start.34 = (f32[512,896]{1,0:T(8,128)S(1)}, f32[512,896]{1,0:T(8,128)S(1)}, u32[]{:S(2)}, u32[]{:S(2)}) collective-permute-start(f32[512,896]{1,0:T(8,128)S(1)} %slice.383), channel_id=1, source_target_pairs={{8,0},{12,4},{16,24},{20,28},{9,1},{13,5},{17,25},{21,29},{10,2},{... | collective-permute-start | bytes 5505032 | tf_op jit(solution)/shard_map/ppermute | solution.py:171
  525.8 26.6 %collective-permute-start.24 = (bf16[512,896]{1,0:T(8,128)(2,1)S(1)}, bf16[512,896]{1,0:T(8,128)(2,1)S(1)}, u32[]{:S(2)}, u32[]{:S(2)}) collective-permute-start(bf16[512,896]{1,0:T(8,128)(2,1)S(1)} %collective-permute-done.23), channel_id=1, source_target_pairs={{8,16},{12,20},{9,17},{13,21},{10,18},{14,22},{11,19},{15,23}} | collective-permute-start | bytes 2752520 | tf_op jit(solution)/shard_map/ppermute | solution.py:119
  526.5 25.9 %collective-permute-start.26 = (bf16[512,896]{1,0:T(8,128)(2,1)S(1)}, bf16[512,896]{1,0:T(8,128)(2,1)S(1)}, u32[]{:S(2)}, u32[]{:S(2)}) collective-permute-start(bf16[512,896]{1,0:T(8,128)(2,1)S(1)} %collective-permute-done.25), channel_id=1, source_target_pairs={{16,8},{20,12},{17,9},{21,13},{18,10},{22,14},{19,11},{23,15}} | collective-permute-start | bytes 2752520 | tf_op jit(solution)/shard_map/ppermute | solution.py:122
  550.2 20.1 %collective-permute-start.35 = (bf16[512,896]{1,0:T(8,128)(2,1)S(1)}, bf16[512,896]{1,0:T(8,128)(2,1)S(1)}, u32[]{:S(2)}, u32[]{:S(2)}) collective-permute-start(bf16[512,896]{1,0:T(8,128)(2,1)S(1)} %slice.381), channel_id=1, source_target_pairs={{0,8},{4,12},{8,16},{12,20},{1,9},{5,13},{9,17},{13,21},{2,10},{6,... | collective-permute-start | bytes 2752520 | tf_op jit(solution)/shard_map/ppermute | solution.py:119
  551.7 19.3 %collective-permute-start.37 = (bf16[512,896]{1,0:T(8,128)(2,1)S(1)}, bf16[512,896]{1,0:T(8,128)(2,1)S(1)}, u32[]{:S(2)}, u32[]{:S(2)}) collective-permute-start(bf16[512,896]{1,0:T(8,128)(2,1)S(1)} %slice.381), channel_id=1, source_target_pairs={{16,8},{20,12},{24,16},{28,20},{17,9},{21,13},{25,17},{29,21},{18,... | collective-permute-start | bytes 2752520 | tf_op jit(solution)/shard_map/ppermute | solution.py:122
  561.3 47.6 %collective-permute-start.27 = (bf16[2048,896]{1,0:T(8,128)(2,1)}, bf16[2048,896]{1,0:T(8,128)(2,1)}, u32[]{:S(2)}, u32[]{:S(2)}) collective-permute-start(bf16[2048,896]{1,0:T(8,128)(2,1)} %pad_maximum_fusion.4), channel_id=1, source_target_pairs={{0,4},{4,0},{8,12},{12,8},{16,20},{20,16},{24,28},{28,24},{1,5},{5... | collective-permute-start | bytes 11010056 | tf_op jit(solution)/shard_map/ppermute | solution.py:135
  573.3 47.1 %collective-permute-start.41 = (f32[512,896]{1,0:T(8,128)}, f32[512,896]{1,0:T(8,128)}, u32[]{:S(2)}, u32[]{:S(2)}) collective-permute-start(f32[512,896]{1,0:T(8,128)} %slice.389), channel_id=1, source_target_pairs={{8,0},{12,4},{16,24},{20,28},{9,1},{13,5},{17,25},{21,29},{10,2},{... | collective-permute-start | bytes 5505032 | tf_op jit(solution)/shard_map/ppermute | solution.py:171
  584.5 64.0 %collective-permute-start.39 = (bf16[2048,896]{1,0:T(8,128)(2,1)}, bf16[2048,896]{1,0:T(8,128)(2,1)}, u32[]{:S(2)}, u32[]{:S(2)}) collective-permute-start(bf16[2048,896]{1,0:T(8,128)(2,1)} %pad_maximum_fusion.6), channel_id=1, source_target_pairs={{0,4},{4,0},{8,12},{12,8},{16,20},{20,16},{24,28},{28,24},{1,5},{5... | collective-permute-start | bytes 11010056 | tf_op jit(solution)/shard_map/ppermute | solution.py:135
  620.4 47.2 %collective-permute-start.44 = (bf16[512,896]{1,0:T(8,128)(2,1)S(1)}, bf16[512,896]{1,0:T(8,128)(2,1)S(1)}, u32[]{:S(2)}, u32[]{:S(2)}) collective-permute-start(bf16[512,896]{1,0:T(8,128)(2,1)S(1)} %slice.388), channel_id=1, source_target_pairs={{16,8},{20,12},{24,16},{28,20},{17,9},{21,13},{25,17},{29,21},{18,... | collective-permute-start | bytes 2752520 | tf_op jit(solution)/shard_map/ppermute | solution.py:122
  621.2 45.7 %collective-permute-start.42 = (bf16[512,896]{1,0:T(8,128)(2,1)S(1)}, bf16[512,896]{1,0:T(8,128)(2,1)S(1)}, u32[]{:S(2)}, u32[]{:S(2)}) collective-permute-start(bf16[512,896]{1,0:T(8,128)(2,1)S(1)} %slice.388), channel_id=1, source_target_pairs={{0,8},{4,12},{8,16},{12,20},{1,9},{5,13},{9,17},{13,21},{2,10},{6,... | collective-permute-start | bytes 2752520 | tf_op jit(solution)/shard_map/ppermute | solution.py:119
  646.7 44.0 %collective-permute-start.28 = (f32[512,896]{1,0:T(8,128)S(1)}, f32[512,896]{1,0:T(8,128)S(1)}, u32[]{:S(2)}, u32[]{:S(2)}) collective-permute-start(f32[512,896]{1,0:T(8,128)S(1)} %slice.377), channel_id=1, source_target_pairs={{8,0},{12,4},{16,24},{20,28},{9,1},{13,5},{17,25},{21,29},{10,2},{... | collective-permute-start | bytes 5505032 | tf_op jit(solution)/shard_map/ppermute | solution.py:171
  666.9 26.6 %collective-permute-start.43 = (bf16[512,896]{1,0:T(8,128)(2,1)S(1)}, bf16[512,896]{1,0:T(8,128)(2,1)S(1)}, u32[]{:S(2)}, u32[]{:S(2)}) collective-permute-start(bf16[512,896]{1,0:T(8,128)(2,1)S(1)} %collective-permute-done.42), channel_id=1, source_target_pairs={{8,16},{12,20},{9,17},{13,21},{10,18},{14,22},{11,19},{15,23}} | collective-permute-start | bytes 2752520 | tf_op jit(solution)/shard_map/ppermute | solution.py:119
  667.6 25.9 %collective-permute-start.45 = (bf16[512,896]{1,0:T(8,128)(2,1)S(1)}, bf16[512,896]{1,0:T(8,128)(2,1)S(1)}, u32[]{:S(2)}, u32[]{:S(2)}) collective-permute-start(bf16[512,896]{1,0:T(8,128)(2,1)S(1)} %collective-permute-done.44), channel_id=1, source_target_pairs={{16,8},{20,12},{17,9},{21,13},{18,10},{22,14},{19,11},{23,15}} | collective-permute-start | bytes 2752520 | tf_op jit(solution)/shard_map/ppermute | solution.py:122
  690.7 22.6 %collective-permute-start.50 = (bf16[512,896]{1,0:T(8,128)(2,1)S(1)}, bf16[512,896]{1,0:T(8,128)(2,1)S(1)}, u32[]{:S(2)}, u32[]{:S(2)}) collective-permute-start(bf16[512,896]{1,0:T(8,128)(2,1)S(1)} %slice.394), channel_id=1, source_target_pairs={{16,8},{20,12},{24,16},{28,20},{17,9},{21,13},{25,17},{29,21},{18,... | collective-permute-start | bytes 2752520 | tf_op jit(solution)/shard_map/ppermute | solution.py:122
  691.5 21.2 %collective-permute-start.48 = (bf16[512,896]{1,0:T(8,128)(2,1)S(1)}, bf16[512,896]{1,0:T(8,128)(2,1)S(1)}, u32[]{:S(2)}, u32[]{:S(2)}) collective-permute-start(bf16[512,896]{1,0:T(8,128)(2,1)S(1)} %slice.394), channel_id=1, source_target_pairs={{0,8},{4,12},{8,16},{12,20},{1,9},{5,13},{9,17},{13,21},{2,10},{6,... | collective-permute-start | bytes 2752520 | tf_op jit(solution)/shard_map/ppermute | solution.py:119
  701.2 23.4 %collective-permute-start.46 = (bf16[2048,896]{1,0:T(8,128)(2,1)S(1)}, bf16[2048,896]{1,0:T(8,128)(2,1)S(1)}, u32[]{:S(2)}, u32[]{:S(2)}) collective-permute-start(bf16[2048,896]{1,0:T(8,128)(2,1)S(1)} %pad_maximum_fusion.7), channel_id=1, source_target_pairs={{0,4},{4,0},{8,12},{12,8},{16,20},{20,16},{24,28},{28,24},{1,5},{5... | collective-permute-start | bytes 11010056 | tf_op jit(solution)/shard_map/ppermute | solution.py:135
  723.3 113.0 %collective-permute-start.40 = (f32[512,896]{1,0:T(8,128)}, f32[512,896]{1,0:T(8,128)}, u32[]{:S(2)}, u32[]{:S(2)}) collective-permute-start(f32[512,896]{1,0:T(8,128)} %slice.384), channel_id=1, source_target_pairs={{8,0},{12,4},{16,24},{20,28},{9,1},{13,5},{17,25},{21,29},{10,2},{... | collective-permute-start | bytes 5505032 | tf_op jit(solution)/shard_map/ppermute | solution.py:171
  739.1 93.1 %collective-permute-start.47 = (f32[512,896]{1,0:T(8,128)}, f32[512,896]{1,0:T(8,128)}, u32[]{:S(2)}, u32[]{:S(2)}) collective-permute-start(f32[512,896]{1,0:T(8,128)} %slice.390), channel_id=1, source_target_pairs={{8,0},{12,4},{16,24},{20,28},{9,1},{13,5},{17,25},{21,29},{10,2},{... | collective-permute-start | bytes 5505032 | tf_op jit(solution)/shard_map/ppermute | solution.py:171
  754.9 116.5 %collective-permute-start.53 = (f32[512,896]{1,0:T(8,128)}, f32[512,896]{1,0:T(8,128)}, u32[]{:S(2)}, u32[]{:S(2)}) collective-permute-start(f32[512,896]{1,0:T(8,128)} %slice.395), channel_id=1, source_target_pairs={{8,0},{12,4},{16,24},{20,28},{9,1},{13,5},{17,25},{21,29},{10,2},{... | collective-permute-start | bytes 5505032 | tf_op jit(solution)/shard_map/ppermute | solution.py:171
  (68 other events, 1623.8 us)
Sparse Core Ops, SparseCore 0:
  67.4 88.1 all-gather.4
  308.2 158.7 all-gather.6
